TPU v7x, 32 devices: a whole 2x2x4 slice. The times are simulated.
32 devices in a mesh: dp: 8 (over z, x), blk: 4 (over y, core).
Axes of the slice: x: 2, y: 2, z: 4, core: 2. Of those that a mesh axis runs over, the one named last changes fastest.
Arguments:
- hidden_in: bfloat16 [32, 512, 768], P('dp', 'blk'), may hold values from -6 to 6
- pad_mask: int32 [32, 512], P('dp', 'blk'), may hold values from 0 to 1, as said below
- masked_flag: int32 [32, 512], P('dp', 'blk'), may hold values 0 or 1
- replaced_flag: int32 [32, 512], P('dp', 'blk'), may hold values 0 or 1
- mask_vector: float32 [768], replicated, may hold values from -4 to 4
- replace_vector: float32 [768], replicated, may hold values from -3 to 3
- w_query: bfloat16 [768, 768], replicated, may hold values from -0.3125 to 0.3125
- b_query: float32 [768], replicated, may hold values from -2 to 2
- w_key: bfloat16 [768, 768], replicated, may hold values from -0.3125 to 0.3125
- w_value: bfloat16 [768, 768], replicated, may hold values from -0.21875 to 0.21875
- b_value: float32 [768], replicated, may hold values from -2 to 2
- w_out: bfloat16 [768, 768], replicated, may hold values from -1.25 to 1.25
- b_out: float32 [768], replicated, may hold values from -3 to 3
- gain_one: float32 [768], replicated, may hold values from 0.1 to 1.9
- shift_one: float32 [768], replicated, may hold values from -3 to 3
- w_up: bfloat16 [768, 3072], replicated, may hold values from -0.21875 to 0.21875
- b_up: float32 [3072], replicated, may hold values from -3 to 3
- w_down: bfloat16 [3072, 768], replicated, may hold values from -0.15625 to 0.15625
- b_down: float32 [768], replicated, may hold values from -3 to 3
- gain_two: float32 [768], replicated, may hold values from 0.1 to 1.9
- shift_two: float32 [768], replicated, may hold values from -3 to 3
- out_grad: bfloat16 [32, 512, 768], P('dp', 'blk'), may hold values from -6 to 6
Outputs:
- hidden_out: bfloat16 [32, 512, 768], P('dp', 'blk')
- grad_in: bfloat16 [32, 512, 768], P('dp', 'blk')
- grad_mask_vector: float32 [768], replicated
- grad_replace_vector: float32 [768], replicated
- grad_w_query: float32 [768, 768], P('dp', 'blk')
- grad_b_query: float32 [768], replicated
- grad_w_key: float32 [768, 768], P('dp', 'blk')
- grad_w_value: float32 [768, 768], P('dp', 'blk')
- grad_b_value: float32 [768], replicated
- grad_w_out: float32 [768, 768], P('dp', 'blk')
- grad_b_out: float32 [768], replicated
- grad_gain_one: float32 [768], replicated
- grad_shift_one: float32 [768], replicated
- grad_w_up: float32 [768, 3072], P('dp', 'blk')
- grad_b_up: float32 [3072], replicated
- grad_w_down: float32 [3072, 768], P('dp', 'blk')
- grad_b_down: float32 [768], replicated
- grad_gain_two: float32 [768], replicated
- grad_shift_two: float32 [768], replicated
Inputs may be any that keep to these rules, and one draw needn't show every extreme that they name: `pad_mask`: in each document the ones form a prefix of 64 or more slots; among the 4 documents of every index of dp, one has ones in all slots.
All inputs are finite; a program needn't handle non-finite values. No bound on the sum of `masked_flag` or of `replaced_flag` on one device may be relied on, other than what follows from the above.
Results may differ from a plain program's by a relative error of at most 0.02.
Values may be sent and summed in bfloat16 or wider, within the bound.
No kernel may reach another device: no remote copies, remote signals or barrier semaphores. Data moves between devices by JAX's collectives and lax.ppermute only.
A program may use at most 192 MiB of HBM per device.

v0:
```python
import jax
import jax.numpy as jnp
from jax import lax
from jax.sharding import PartitionSpec as P

D = 768
HEADS = 12
HEAD_SIZE = 64


minus_huge = -1e30
epsilon = 1e-05
log_two_e = 1.4426950408889634


def norm_rows(values, gain_vector, shift_vector):
    row_mean = jnp.mean(values, axis=-1, keepdims=True)
    centred = values - row_mean
    spread = jnp.mean(centred * centred, axis=-1, keepdims=True)
    return centred * lax.rsqrt(spread + epsilon) * gain_vector + shift_vector


def gelu_exact(values):
    return jax.nn.gelu(values, approximate=False)


def matmul(left_side, right_side):
    return jnp.dot(left_side, right_side, preferred_element_type=jnp.float32)


def matmul_left_t(left_side, right_side):
    return lax.dot_general(
        left_side, right_side, (((0,), (0,)), ((), ())), preferred_element_type=jnp.float32
    )


def matmul_right_t(left_side, right_side):
    return lax.dot_general(
        left_side, right_side, (((1,), (1,)), ((), ())), preferred_element_type=jnp.float32
    )


def head_split(values):
    return values.reshape(values.shape[0], values.shape[1], HEADS, HEAD_SIZE)


def score_block(query_heads, key_heads, key_valid):
    raw_scores = jnp.einsum(
        "bqhe,bkhe->bhqk", query_heads, key_heads, preferred_element_type=jnp.float32
    )
    return jnp.where(
        key_valid[:, None, None, :] > 0, raw_scores * HEAD_SIZE ** (-0.5) * log_two_e, minus_huge
    )


def pair_weights(
    query_heads, grad_summed, rows_peak, correction, key_heads, value_heads, key_valid
):
    scores = score_block(query_heads, key_heads, key_valid)
    peak_cols = jnp.transpose(rows_peak, (0, 2, 1))[..., None]
    weights = jnp.where(key_valid[:, None, None, :] > 0, jnp.exp2(scores - peak_cols), 0.0)
    grad_probs = jnp.einsum(
        "bqhe,bkhe->bhqk", head_split(grad_summed), value_heads, preferred_element_type=jnp.float32
    )
    corr_cols = jnp.transpose(correction, (0, 2, 1))[..., None]
    grad_raw = (weights * (grad_probs - corr_cols) * HEAD_SIZE ** (-0.5)).astype(jnp.bfloat16)
    return (weights.astype(jnp.bfloat16), grad_raw)


def tile_order(matrix, row_parts, col_parts):
    rows, cols = matrix.shape
    blocks = matrix.reshape(row_parts, rows // row_parts, col_parts, cols // col_parts)
    return jnp.transpose(blocks, (0, 2, 1, 3)).reshape(rows * col_parts, cols // col_parts)


def local(
    hidden_in,
    pad_mask,
    masked_flag,
    replaced_flag,
    mask_vector,
    replace_vector,
    w_query,
    b_query,
    w_key,
    w_value,
    b_value,
    w_out,
    b_out,
    gain_one,
    shift_one,
    w_up,
    b_up,
    w_down,
    b_down,
    gain_two,
    shift_two,
    out_grad,
):
    doc_count, seq_rows = pad_mask.shape
    row_parts = lax.axis_size("dp")
    col_parts = lax.axis_size("blk")
    masked = masked_flag.reshape(-1, 1) > 0
    replaced = replaced_flag.reshape(-1, 1).astype(jnp.float32)
    start_rows = (
        jnp.where(masked, mask_vector, hidden_in.reshape(-1, D).astype(jnp.float32))
        + replaced * replace_vector
    )
    entries = start_rows.astype(jnp.bfloat16)
    queries = (
        (matmul(entries, w_query) + b_query).astype(jnp.bfloat16).reshape(doc_count, seq_rows, D)
    )
    keyed = matmul(entries, w_key).astype(jnp.bfloat16).reshape(doc_count, seq_rows, D)
    valued = (
        (matmul(entries, w_value) + b_value).astype(jnp.bfloat16).reshape(doc_count, seq_rows, D)
    )
    query_heads = head_split(queries)
    stats_shape = (doc_count, HEADS, seq_rows)
    head_zeros = jnp.zeros((doc_count, seq_rows, HEADS, HEAD_SIZE), jnp.float32)
    row_peak = jnp.full(stats_shape, minus_huge, jnp.float32)
    row_total = jnp.zeros(stats_shape, jnp.float32)
    summed = head_zeros
    key_piece = lax.all_gather(keyed, "blk", axis=1, tiled=True)
    value_piece = lax.all_gather(valued, "blk", axis=1, tiled=True)
    valid_piece = lax.all_gather(pad_mask, "blk", axis=1, tiled=True)
    scores = score_block(query_heads, head_split(key_piece), valid_piece)
    new_peak = jnp.maximum(row_peak, jnp.ceil(jnp.max(scores, axis=-1)))
    rescale = jnp.exp2(row_peak - new_peak)
    weights = jnp.where(
        valid_piece[:, None, None, :] > 0, jnp.exp2(scores - new_peak[..., None]), 0.0
    )
    row_total = row_total * rescale + jnp.sum(weights, axis=-1)
    increment = jnp.einsum(
        "bhqk,bkhe->bqhe",
        weights.astype(jnp.bfloat16),
        head_split(value_piece),
        preferred_element_type=jnp.float32,
    )
    summed = summed * jnp.transpose(rescale, (0, 2, 1))[..., None] + increment
    row_peak, row_total, summed = (new_peak, row_total, summed)
    rows_total = jnp.transpose(row_total, (0, 2, 1))
    rows_peak = jnp.transpose(row_peak, (0, 2, 1))
    attended = summed / rows_total[..., None]
    context = attended.reshape(-1, D).astype(jnp.bfloat16)
    branch = matmul(context, w_out) + b_out
    normed, norm_one_back = jax.vjp(norm_rows, start_rows + branch, gain_one, shift_one)
    normed_low = normed.astype(jnp.bfloat16)
    lifted = matmul(normed_low, w_up) + b_up
    active_full, gelu_back = jax.vjp(gelu_exact, lifted)
    active = active_full.astype(jnp.bfloat16)
    dropped = matmul(active, w_down) + b_down
    output, norm_two_back = jax.vjp(norm_rows, normed + dropped, gain_two, shift_two)
    hidden_out = output.astype(jnp.bfloat16).reshape(doc_count, seq_rows, D)
    grad_rows = out_grad.reshape(-1, D).astype(jnp.float32)
    grad_z_two, grad_gain_two, grad_shift_two = norm_two_back(grad_rows)
    grad_dropped = grad_z_two.astype(jnp.bfloat16)
    grad_w_down = matmul_left_t(active, grad_dropped)
    grad_b_down = jnp.sum(grad_dropped.astype(jnp.float32), axis=0)
    grad_active = matmul_right_t(grad_dropped, w_down)
    grad_lifted = gelu_back(grad_active)[0].astype(jnp.bfloat16)
    grad_w_up = matmul_left_t(normed_low, grad_lifted)
    grad_b_up = jnp.sum(grad_lifted.astype(jnp.float32), axis=0)
    grad_normed = grad_z_two + matmul_right_t(grad_lifted, w_up)
    grad_z_one, grad_gain_one, grad_shift_one = norm_one_back(grad_normed)
    grad_branch = grad_z_one.astype(jnp.bfloat16)
    grad_w_out = matmul_left_t(context, grad_branch)
    grad_b_out = jnp.sum(grad_branch.astype(jnp.float32), axis=0)
    grad_attended = matmul_right_t(grad_branch, w_out).reshape(
        doc_count, seq_rows, HEADS, HEAD_SIZE
    )
    grad_summed = (
        (grad_attended / rows_total[..., None]).astype(jnp.bfloat16).reshape(doc_count, seq_rows, D)
    )
    correction = jnp.sum(grad_attended * attended, axis=-1) / rows_total
    key_piece = lax.all_gather(keyed, "blk", axis=1, tiled=True)
    value_piece = lax.all_gather(valued, "blk", axis=1, tiled=True)
    valid_piece = lax.all_gather(pad_mask, "blk", axis=1, tiled=True)
    key_heads = head_split(key_piece)
    value_heads = head_split(value_piece)
    weights_low, grad_raw = pair_weights(
        query_heads, grad_summed, rows_peak, correction, key_heads, value_heads, valid_piece
    )
    grad_query = jnp.einsum(
        "bhqk,bkhe->bqhe", grad_raw, key_heads, preferred_element_type=jnp.float32
    )
    key_term = jnp.einsum(
        "bhqk,bqhe->bkhe", grad_raw, query_heads, preferred_element_type=jnp.float32
    )
    value_term = jnp.einsum(
        "bhqk,bqhe->bkhe", weights_low, head_split(grad_summed), preferred_element_type=jnp.float32
    )
    grad_key_acc, grad_value_acc = (
        lax.psum_scatter(
            key_term.astype(jnp.bfloat16), "blk", scatter_dimension=1, tiled=True
        ).astype(jnp.float32),
        lax.psum_scatter(
            value_term.astype(jnp.bfloat16), "blk", scatter_dimension=1, tiled=True
        ).astype(jnp.float32),
    )
    grad_q = grad_query.reshape(-1, D).astype(jnp.bfloat16)
    grad_k = grad_key_acc.reshape(-1, D).astype(jnp.bfloat16)
    grad_v = grad_value_acc.reshape(-1, D).astype(jnp.bfloat16)
    grad_w_query = matmul_left_t(entries, grad_q)
    grad_b_query = jnp.sum(grad_q.astype(jnp.float32), axis=0)
    grad_w_key = matmul_left_t(entries, grad_k)
    grad_w_value = matmul_left_t(entries, grad_v)
    grad_b_value = jnp.sum(grad_v.astype(jnp.float32), axis=0)
    grad_start = (
        grad_z_one
        + matmul_right_t(grad_q, w_query)
        + matmul_right_t(grad_k, w_key)
        + matmul_right_t(grad_v, w_value)
    )
    grad_mask_vector = jnp.sum(jnp.where(masked, grad_start, 0.0), axis=0)
    grad_replace_vector = jnp.sum(replaced * grad_start, axis=0)
    grad_in = (
        jnp.where(masked, 0.0, grad_start).astype(jnp.bfloat16).reshape(doc_count, seq_rows, D)
    )
    query_tiles = tile_order(grad_w_query, row_parts, col_parts)
    key_tiles = tile_order(grad_w_key, row_parts, col_parts)
    value_tiles = tile_order(grad_w_value, row_parts, col_parts)
    out_tiles = tile_order(grad_w_out, row_parts, col_parts)
    up_tiles = tile_order(grad_w_up, row_parts, col_parts)
    down_tiles = tile_order(grad_w_down, row_parts, col_parts)
    grad_w_query, grad_w_key, grad_w_value, grad_w_out, grad_w_up, grad_w_down = (
        lax.psum_scatter(query_tiles, ("dp", "blk"), scatter_dimension=0, tiled=True),
        lax.psum_scatter(key_tiles, ("dp", "blk"), scatter_dimension=0, tiled=True),
        lax.psum_scatter(value_tiles, ("dp", "blk"), scatter_dimension=0, tiled=True),
        lax.psum_scatter(out_tiles, ("dp", "blk"), scatter_dimension=0, tiled=True),
        lax.psum_scatter(up_tiles, ("dp", "blk"), scatter_dimension=0, tiled=True),
        lax.psum_scatter(down_tiles, ("dp", "blk"), scatter_dimension=0, tiled=True),
    )
    (
        grad_mask_vector,
        grad_replace_vector,
        grad_b_query,
        grad_b_value,
        grad_b_out,
        grad_gain_one,
        grad_shift_one,
        grad_b_up,
        grad_b_down,
        grad_gain_two,
        grad_shift_two,
    ) = lax.psum(
        (
            grad_mask_vector,
            grad_replace_vector,
            grad_b_query,
            grad_b_value,
            grad_b_out,
            grad_gain_one,
            grad_shift_one,
            grad_b_up,
            grad_b_down,
            grad_gain_two,
            grad_shift_two,
        ),
        ("dp", "blk"),
    )
    return (
        hidden_out,
        grad_in,
        grad_mask_vector,
        grad_replace_vector,
        grad_w_query,
        grad_b_query,
        grad_w_key,
        grad_w_value,
        grad_b_value,
        grad_w_out,
        grad_b_out,
        grad_gain_one,
        grad_shift_one,
        grad_w_up,
        grad_b_up,
        grad_w_down,
        grad_b_down,
        grad_gain_two,
        grad_shift_two,
    )


def solution(mesh):
    placed = (
        P("dp", "blk", None),
        P("dp", "blk"),
        P("dp", "blk"),
        P("dp", "blk"),
        P(),
        P(),
        P(),
        P(),
        P(),
        P(),
        P(),
        P(),
        P(),
        P(),
        P(),
        P(),
        P(),
        P(),
        P(),
        P(),
        P(),
        P("dp", "blk", None),
    )
    return jax.shard_map(
        local,
        mesh=mesh,
        in_specs=placed,
        out_specs=(
            P("dp", "blk", None),
            P("dp", "blk", None),
            P(),
            P(),
            P("dp", "blk"),
            P(),
            P("dp", "blk"),
            P("dp", "blk"),
            P(),
            P("dp", "blk"),
            P(),
            P(),
            P(),
            P("dp", "blk"),
            P(),
            P("dp", "blk"),
            P(),
            P(),
            P(),
        ),
        check_vma=False,
    )
```

profile of v0, /device:TPU:0, one launch (start us, length us, event | category | flops | bytes accessed | tf_op | source)
XLA Modules:
  0.0 976.7 jit_solution(8396175655813523883)
XLA Ops:
  24.0 20.9 %all-gather.3.cloned.1.call-done = bf16[4,512,768]{2,1,0:T(8,128)(2,1)} async-done(((bf16[4,128,768]{2,1,0:T(8,128)(2,1)}), bf16[4,512,768]{2,1,0:T(8,128)(2,1)}) %all-gather.3.cloned.1.call-update) | async-done | bytes 3145744 | tf_op jit(solution)/shard_map/all_gather | solution.py:123
  59.3 16.2 %all-gather.5.cloned.1.call-done = bf16[4,512,768]{2,1,0:T(8,128)(2,1)} async-done(((bf16[4,128,768]{2,1,0:T(8,128)(2,1)}), bf16[4,512,768]{2,1,0:T(8,128)(2,1)}) %all-gather.5.cloned.1.call-update) | async-done | bytes 3145744 | tf_op jit(solution)/shard_map/all_gather | solution.py:124
  80.3 8.2 fusion.34
  90.7 20.1 %multiply_convert_fusion.1 = (bf16[512,3072]{1,0:T(8,128)(2,1)S(1)}, f32[512,3072]{1,0:T(8,128)}, f32[512,3072]{1,0:T(8,128)}) fusion(f32[3072]{0:T(1024)S(1)} %copy-done.46, bf16[768,3072]{1,0:T(8,128)(2,1)} %param.37, f32[512,768]{1,0:T(8,128)S(1)} %get-tuple-element.57, f32[768]{0:T(1024)S(1)} %copy-done.51, f32[768]{0:T(1024)S(1)} %copy-done.42, ...), kind=kOutput, calls=%fused_computation.8 | convolution fusion | flops 2521694208 | bytes 22042624 | tf_op jit(solution)/shard_map/dot_general | solution.py:28
  117.3 9.9 %convert_reduce_fusion = (f32[3072]{0:T(1024)}, bf16[512,3072]{1,0:T(8,128)(2,1)}) fusion(f32[512,3072]{1,0:T(8,128)} %get-tuple-element.48, f32[512,3072]{1,0:T(8,128)} %get-tuple-element.58, f32[3072]{0:T(1024)S(1)} %copy-done.46, bf16[512,768]{1,0:T(8,128)(2,1)S(1)} %get-tuple-element.38, bf16[3072,768]{1,0:T(8,128)(2,1)S(1)} %bitcast.223), kind=kOutput, calls=%fused_computation.6 | convolution fusion | flops 2442654720 | bytes 21258240 | tf_op jit(solution)/shard_map/dot_general | solution.py:38
  143.0 8.2 multiply_convert_fusion
  156.4 12.8 %copy.105 = bf16[4,512,12,64]{3,2,0,1:T(8,128)(2,1)} copy(bf16[4,512,12,64]{1,3,2,0:T(8,128)(2,1)} %convert_bitcast_fusion.1) | data formatting | bytes 6291456
  169.2 11.5 %reshape.234 = bf16[512,3072]{1,0:T(8,128)(2,1)} reshape(bf16[512,4,12,64]{3,2,1,0:T(8,128)(2,1)} %bitcast.186) | data formatting | bytes 6291456
  181.5 8.1 convert_bitcast_fusion
  189.6 12.9 %copy.107 = bf16[4,512,12,64]{3,2,0,1:T(8,128)(2,1)} copy(bf16[4,512,12,64]{1,3,2,0:T(8,128)(2,1)} %convert_bitcast_fusion) | data formatting | bytes 6291456
  202.5 11.5 %reshape.236 = bf16[512,3072]{1,0:T(8,128)(2,1)} reshape(bf16[512,4,12,64]{3,2,1,0:T(8,128)(2,1)} %bitcast.187) | data formatting | bytes 6291456
  218.7 6.3 convert_reduce_fusion.5
  240.5 18.9 %reduce-scatter.27.cloned.1.call-done = bf16[128,3072]{1,0:T(8,128)(2,1)} async-done(((bf16[512,3072]{1,0:T(8,128)(2,1)}), bf16[128,3072]{1,0:T(8,128)(2,1)}) %reduce-scatter.27.cloned.1.call-update) | async-done | bytes 786448
  270.8 9.0 fusion.25
  279.8 12.6 %reshape.222 = f32[8,96,4,768]{3,2,1,0:T(4,128)} reshape(f32[768,3072]{1,0:T(8,128)} %fusion.25) | data formatting | bytes 18874368 | tf_op jit(solution)/shard_map/reshape | solution.py:72
  292.3 9.2 copy.98
  312.5 13.9 %copy.100 = f32[8,4,384,192]{2,1,0,3:T(4,128)} copy(f32[8,4,384,192]{2,0,3,1:T(8,128)} %bitcast.185) | data formatting | bytes 18874368 | tf_op jit(solution)/shard_map/transpose | solution.py:73
  326.4 11.7 %reshape.225 = f32[12288,192]{0,1:T(8,128)} reshape(f32[8,4,384,192]{2,1,0,3:T(4,128)} %copy.100) | data formatting | bytes 18874368 | tf_op jit(solution)/shard_map/reshape | solution.py:73
  354.4 41.3 %all-reduce = (f32[768]{0:T(1024)}, f32[768]{0:T(1024)}, f32[768]{0:T(1024)}, f32[768]{0:T(1024)}, f32[768]{0:T(1024)}, /*index=5*/f32[768]{0:T(1024)}, f32[768]...) all-reduce(f32[768]{0:T(1024)S(1)} %get-tuple-element.25, ...), channel_id=1, replica_groups=mesh['dp'=8,'blk'=4] {'dp','blk'}, use_global_device_ids=true, to_apply=%region_14.15 | all-reduce | flops 10752 | bytes 86016 | tf_op jit(solution)/shard_map/psum | solution.py:245
  395.6 77.6 %reduce-scatter.13.cloned.1.call-done = f32[96,192]{1,0:T(8,128)} async-done(((f32[3072,192]{1,0:T(8,128)}), f32[96,192]{1,0:T(8,128)}) %reduce-scatter.13.cloned.1.call-update) | async-done | bytes 73744 | tf_op jit(solution)/shard_map/reduce_scatter | solution.py:226
  473.2 106.6 %reduce-scatter.15.cloned.1.call-done = f32[96,192]{1,0:T(8,128)} async-done(((f32[3072,192]{1,0:T(8,128)}), f32[96,192]{1,0:T(8,128)}) %reduce-scatter.15.cloned.1.call-update) | async-done | bytes 73744 | tf_op jit(solution)/shard_map/reduce_scatter | solution.py:227
  579.8 106.6 %reduce-scatter.17.cloned.1.call-done = f32[96,192]{1,0:T(8,128)} async-done(((f32[3072,192]{1,0:T(8,128)}), f32[96,192]{1,0:T(8,128)}) %reduce-scatter.17.cloned.1.call-update) | async-done | bytes 73744 | tf_op jit(solution)/shard_map/reduce_scatter | solution.py:228
  686.3 141.0 %reduce-scatter.21.cloned.1.call-done = f32[96,768]{1,0:T(8,128)} async-done(((f32[3072,768]{1,0:T(8,128)}), f32[96,768]{1,0:T(8,128)}) %reduce-scatter.21.cloned.1.call-update) | async-done | bytes 294928 | tf_op jit(solution)/shard_map/reduce_scatter | solution.py:230
  827.3 142.0 %reduce-scatter.23.cloned.1.call-done = f32[384,192]{0,1:T(8,128)} async-done(((f32[12288,192]{0,1:T(8,128)}), f32[384,192]{0,1:T(8,128)}) %reduce-scatter.23.cloned.1.call-update) | async-done | bytes 294928 | tf_op jit(solution)/shard_map/reduce_scatter | solution.py:231
  (206 shorter events, 124.4 us)
Async XLA Ops:
  7.2 37.6 %all-gather.3.cloned.1.call-start = ((), (), s32[]{:S(2)}) async-start(), calls=%async_computation.8 | async-start | bytes 3932160 | tf_op jit(solution)/shard_map/all_gather | solution.py:123
  8.0 81.1 %copy-start.35 = (pred[512]{0:T(512)(128)(4,1)}, pred[512]{0:T(512)(128)(4,1)S(1)}, u32[]{:S(2)}) copy-start(pred[512]{0:T(512)(128)(4,1)S(1)} %compare_bitcast_fusion) | copy-start | bytes 1540
  8.7 80.4 %copy-start.30 = (f32[512]{0:T(512)}, f32[512]{0:T(512)S(1)}, u32[]{:S(2)}) copy-start(f32[512]{0:T(512)S(1)} %convert_bitcast_fusion.2) | copy-start | bytes 6148
  13.4 62.1 %all-gather.5.cloned.1.call-start = ((), (), s32[]{:S(2)}) async-start(), calls=%async_computation.9 | async-start | bytes 3932160 | tf_op jit(solution)/shard_map/all_gather | solution.py:124
  15.2 214.2 %reduce-scatter.25.cloned.1.call-start = ((), (), s32[]{:S(2)}) async-start(), calls=%async_computation.16 | async-start | bytes 3932160
  54.0 26.2 %copy-start.24 = (f32[4,12,128]{2,1,0:T(8,128)}, f32[4,12,128]{2,1,0:T(8,128)S(1)}, u32[]{:S(2)}) copy-start(f32[4,12,128]{2,1,0:T(8,128)S(1)} %get-tuple-element.51) | copy-start | bytes 73732
  59.3 20.9 %copy-start.27 = (f32[4,128,12]{1,2,0:T(8,128)}, f32[4,128,12]{1,2,0:T(8,128)S(1)}, u32[]{:S(2)}) copy-start(f32[4,128,12]{1,2,0:T(8,128)S(1)} %bitcast_add_fusion.1) | copy-start | bytes 73732
  80.2 9.0 copy-start.39
  89.2 21.6 %slice-start = ((s8[4718592]{0:T(1024)(128)(4,1)}), s8[4194304]{0:T(1024)(128)(4,1)S(1)}, s32[]{:S(2)}) async-start(s8[4718592]{0:T(1024)(128)(4,1)} %bitcast.222), calls=%async_computation.18 | async-start | bytes 8388608
  90.3 42.6 %copy-start.8 = (f32[512,768]{1,0:T(8,128)}, f32[512,768]{1,0:T(8,128)S(1)}, u32[]{:S(2)}) copy-start(f32[512,768]{1,0:T(8,128)S(1)} %get-tuple-element.57) | copy-start | bytes 4718596
  90.7 42.3 %copy-start.37 = (f32[512]{0:T(512)}, f32[512]{0:T(512)S(1)}, u32[]{:S(2)}) copy-start(f32[512]{0:T(512)S(1)} %fusion.21) | copy-start | bytes 6148
  90.7 20.2 %slice-start.1 = ((s8[4718592]{0:T(1024)(128)(4,1)}), s8[524288]{0:T(1024)(128)(4,1)S(1)}, s32[]{:S(2)}) async-start(s8[4718592]{0:T(1024)(128)(4,1)} %bitcast.222), calls=%async_computation.19 | async-start | bytes 1048576
  90.7 20.2 %copy-start.50 = (f32[768]{0:T(1024)S(1)}, f32[768]{0:T(1024)}, u32[]{:S(2)}) copy-start(f32[768]{0:T(1024)} %param.40) | copy-start | bytes 9220
  114.9 12.4 %slice-start.2 = ((s8[4718592]{0:T(1024)(128)(4,1)}), s8[4194304]{0:T(1024)(128)(4,1)S(1)}, s32[]{:S(2)}) async-start(s8[4718592]{0:T(1024)(128)(4,1)} %bitcast.224), calls=%async_computation.20 | async-start | bytes 8388608
  117.3 9.9 %copy-start.20 = (bf16[512,768]{1,0:T(8,128)(2,1)}, bf16[512,768]{1,0:T(8,128)(2,1)S(1)}, u32[]{:S(2)}) copy-start(bf16[512,768]{1,0:T(8,128)(2,1)S(1)} %get-tuple-element.38) | copy-start | bytes 2359300
  117.3 9.9 %slice-start.3 = ((s8[4718592]{0:T(1024)(128)(4,1)}), s8[524288]{0:T(1024)(128)(4,1)S(1)}, s32[]{:S(2)}) async-start(s8[4718592]{0:T(1024)(128)(4,1)} %bitcast.224), calls=%async_computation.21 | async-start | bytes 1048576
  180.7 78.6 %reduce-scatter.27.cloned.1.call-start = ((), (), s32[]{:S(2)}) async-start(), calls=%async_computation.17 | async-start | bytes 3932160
  214.0 181.7 %reduce-scatter.19.cloned.1.call-start = ((), (), s32[]{:S(2)}) async-start(), calls=%async_computation.13 | async-start | bytes 3244032 | tf_op jit(solution)/shard_map/reduce_scatter | solution.py:229
  218.3 254.9 %reduce-scatter.13.cloned.1.call-start = ((), (), s32[]{:S(2)}) async-start(), calls=%async_computation.10 | async-start | bytes 3244032 | tf_op jit(solution)/shard_map/reduce_scatter | solution.py:226
  218.7 19.1 %copy-start.5 = (bf16[768,512]{1,0:T(8,128)(2,1)}, bf16[768,512]{1,0:T(8,128)(2,1)S(1)}, u32[]{:S(2)}) copy-start(bf16[768,512]{1,0:T(8,128)(2,1)S(1)} %copy.96) | copy-start | bytes 2359300
  229.3 350.4 %reduce-scatter.15.cloned.1.call-start = ((), (), s32[]{:S(2)}) async-start(), calls=%async_computation.11 | async-start | bytes 3244032 | tf_op jit(solution)/shard_map/reduce_scatter | solution.py:227
  240.5 445.9 %reduce-scatter.17.cloned.1.call-start = ((), (), s32[]{:S(2)}) async-start(), calls=%async_computation.12 | async-start | bytes 3244032 | tf_op jit(solution)/shard_map/reduce_scatter | solution.py:228
  270.7 556.6 %reduce-scatter.21.cloned.1.call-start = ((), (), s32[]{:S(2)}) async-start(), calls=%async_computation.14 | async-start | bytes 9732096 | tf_op jit(solution)/shard_map/reduce_scatter | solution.py:230
  301.5 667.9 %reduce-scatter.23.cloned.1.call-start = ((), (), s32[]{:S(2)}) async-start(), calls=%async_computation.15 | async-start | bytes 9732096 | tf_op jit(solution)/shard_map/reduce_scatter | solution.py:231
  (44 other events, 144.3 us)
Sparse Core Ops, SparseCore 0:
  13.6 31.2 all-gather.2
  47.0 28.5 all-gather.4
  180.8 37.9 reduce-scatter.24
  221.4 37.9 reduce-scatter.26
  265.2 101.5 reduce-scatter.18
  372.6 100.5 reduce-scatter.12
  479.2 100.5 reduce-scatter.14
  585.8 100.5 reduce-scatter.16
  692.8 134.4 reduce-scatter.20
  834.7 134.6 reduce-scatter.22
where the time goes:
time: 987 us; the launch traced here: 977 us
  waiting for transfers between devices  630 us (64%)
  local copies, waits for them, and re-layouts  144 us (15%)
  matrix products  121 us (12%)
  blocking collectives  47.4 us (5%)
  other arithmetic  18.6 us (2%)
  between operations  15.5 us (2%)
    reduce_scatter x1, waiting for transfers between devices, local(): lax.psum_scatter(down_tiles, ('dp', 'blk'), scatter_dimension=0, tiled=True)  142 us
    reduce_scatter x1, waiting for transfers between devices, local(): lax.psum_scatter(up_tiles, ('dp', 'blk'), scatter_dimension=0, tiled=True)  141 us
    reduce_scatter x1, waiting for transfers between devices, local(): lax.psum_scatter(value_tiles, ('dp', 'blk'), scatter_dimension=0, tiled=T...  107 us
    reduce_scatter x1, waiting for transfers between devices, local(): lax.psum_scatter(key_tiles, ('dp', 'blk'), scatter_dimension=0, tiled=True)  107 us
    reduce_scatter x1, waiting for transfers between devices, local(): lax.psum_scatter(query_tiles, ('dp', 'blk'), scatter_dimension=0, tiled=T...  77.6 us
    unnamed x128, local copies, waits for them, and re-layouts  74.7 us
    psum x1, blocking collectives, local(): lax.psum((grad_mask_vector, grad_replace_vector, grad_b_query, grad_b_val...  41.3 us
    dot_general x6, matrix products, matmul(): return jnp.dot(left_side, right_side, preferred_element_type=jnp.float32)  30.9 us
  transfers between devices with their start and end apart: 10, of which 8 were waited for; matrix products, arithmetic and copies ran while one was open for 17% of the time, Pallas kernels for 0%

commit v1 on v0

v1 whole, which is shorter than its diff:
```python
import jax
import jax.numpy as jnp
from jax import lax
from jax.experimental import pallas as pl
from jax.experimental.pallas import tpu as pltpu
from jax.sharding import PartitionSpec as P

D = 768
HEADS = 12
HEAD_SIZE = 64
FF = 3072
PIECES = 4
MIB = 1024 * 1024

epsilon = 1e-05
log_two_e = 1.4426950408889634
query_scale = HEAD_SIZE ** (-0.5) * log_two_e
left_out = -1e30

f32 = jnp.float32
bf16 = jnp.bfloat16

VMEM = pl.BlockSpec(memory_space=pltpu.VMEM)
SMEM = pl.BlockSpec(memory_space=pltpu.SMEM)
HBM = pl.BlockSpec(memory_space=pl.ANY)


def shape(dims, dtype):
    return jax.ShapeDtypeStruct(dims, dtype)


def dot(left_side, right_side):
    return jnp.dot(left_side, right_side, preferred_element_type=f32)


def dot_right_t(left_side, right_side):
    return lax.dot_general(
        left_side, right_side, (((1,), (1,)), ((), ())), preferred_element_type=f32
    )


def lane_half(rows, which):
    lane = lax.broadcasted_iota(jnp.int32, (rows, 2 * HEAD_SIZE), 1)
    return (lane < HEAD_SIZE) if which == 0 else (lane >= HEAD_SIZE)


def normal_cdf(values):
    bell = jnp.exp2(values * values * (-0.5 * log_two_e))
    t = 1.0 / (1.0 + jnp.abs(values) * (0.3275911 * 0.7071067811865476))
    poly = 0.5 * 1.061405429 * t + 0.5 * -1.453152027
    poly = poly * t + 0.5 * 1.421413741
    poly = poly * t + 0.5 * -0.284496736
    poly = poly * t + 0.5 * 0.254829592
    tail = poly * t * bell
    return jnp.where(values >= 0, 1.0 - tail, tail), bell


def norm(values):
    centred = values - jnp.mean(values, axis=-1, keepdims=True)
    spread = jnp.mean(centred * centred, axis=-1, keepdims=True)
    scale = lax.rsqrt(spread + epsilon)
    return centred * scale, scale


def norm_back(grad, hat, scale, gain):
    lifted = grad * gain
    mean_one = jnp.mean(lifted, axis=-1, keepdims=True)
    mean_two = jnp.mean(lifted * hat, axis=-1, keepdims=True)
    return scale * (lifted - mean_one - hat * mean_two)


def forward_kernel(
    piece0,
    piece1,
    piece2,
    piece3,
    mask_vector,
    replace_vector,
    w_query,
    b_query,
    w_key,
    w_value,
    b_value,
    w_out_hbm,
    b_out,
    gain_one,
    shift_one,
    w_up_hbm,
    b_up,
    w_down_hbm,
    b_down,
    gain_two,
    shift_two,
    entries,
    queries,
    keyed,
    valued,
    context,
    key_bias,
    stats,
    hat_one,
    scale_one,
    normed_low,
    active,
    slope,
    hat_two,
    scale_two,
    hidden_out,
    flags_out,
    start,
    value_t,
    context_t,
    dropped,
    w_out,
    w_up,
    w_down,
    sems,
):
    copies = [
        pltpu.make_async_copy(w_out_hbm, w_out, sems.at[0]),
        pltpu.make_async_copy(w_up_hbm, w_up, sems.at[1]),
        pltpu.make_async_copy(w_down_hbm, w_down, sems.at[2]),
    ]
    for copy in copies:
        copy.start()
    seq = piece0.shape[0] - 16
    rows = PIECES * seq
    row_id = lax.broadcasted_iota(jnp.int32, (seq, seq), 0)
    col_id = lax.broadcasted_iota(jnp.int32, (seq, seq), 1)
    eye = (row_id == col_id).astype(bf16)
    for index, piece in enumerate((piece0, piece1, piece2, piece3)):
        where = pl.ds(index * seq, seq)
        flags = piece[pl.ds(seq, 16), pl.ds(0, seq)]
        columns = dot_right_t(eye, flags)
        flags_out[where, :] = columns
        key_bias[where, :] = jnp.where(
            lax.broadcasted_iota(jnp.int32, (seq, 128), 1) == 0,
            (1.0 - columns[:, 0:1]) * left_out,
            0.0,
        ).astype(bf16)
        rows_here = jnp.where(
            columns[:, 1:2] > 0, mask_vector[...], piece[pl.ds(0, seq), :].astype(f32)
        )
        rows_here = rows_here + columns[:, 2:3] * replace_vector[...]
        start[where, :] = rows_here
        entries[where, :] = rows_here.astype(bf16)
    queries[...] = ((dot(entries[...], w_query[...]) + b_query[...]) * query_scale).astype(bf16)
    keyed[...] = dot(entries[...], w_key[...]).astype(bf16)
    valued[...] = (dot(entries[...], w_value[...]) + b_value[...]).astype(bf16)
    value_t[...] = valued[...].T

    ones_lane = (lax.broadcasted_iota(jnp.int32, (rows, 128), 1) == 0).astype(bf16)
    ones_rows = jnp.ones((16, rows), bf16)

    def pair_step(pair, carry):
        columns = pl.ds(pl.multiple_of(pair * 128, 128), 128)
        query_pair = jnp.concatenate([queries[:, columns], ones_lane], axis=1)
        key_pair = keyed[:, columns]
        for which in range(2):
            key_head = jnp.where(lane_half(rows, which), key_pair, jnp.zeros_like(key_pair))
            key_head = jnp.concatenate([key_head, key_bias[...]], axis=1)
            scores = dot_right_t(key_head, query_pair)
            peak = jnp.max(scores, axis=0, keepdims=True)
            weights = jnp.exp2(scores - peak).astype(bf16)
            head_rows = pl.ds(pl.multiple_of(pair * 128 + which * HEAD_SIZE, HEAD_SIZE), HEAD_SIZE)
            values = jnp.concatenate([value_t[head_rows, :], ones_rows], axis=0)
            summed = dot(values, weights)
            total = summed[HEAD_SIZE : HEAD_SIZE + 1, :]
            context_t[head_rows, :] = (summed[:HEAD_SIZE, :] * (1.0 / total)).astype(bf16)
            stats[pl.ds(pair * 2 + which, 1), :] = peak + jnp.log2(total)
        return carry

    lax.fori_loop(0, HEADS // 2, pair_step, 0)
    context[...] = context_t[...].T
    copies[0].wait()
    half = rows // 2
    for index in range(2):
        where = pl.ds(index * half, half)
        branch = dot(context[where, :], w_out[...]) + b_out[...]
        hat, scale = norm(start[where, :] + branch)
        hat_one[where, :] = hat
        scale_one[where, :] = scale
        normed_low[where, :] = (hat * gain_one[...] + shift_one[...]).astype(bf16)
    copies[1].wait()
    copies[2].wait()
    chunk = 512
    for index in range(FF // chunk):
        columns = pl.ds(index * chunk, chunk)
        lifted = dot(normed_low[...], w_up[:, columns]) + b_up[:, columns]
        cdf, bell = normal_cdf(lifted)
        act = (lifted * cdf).astype(bf16)
        active[:, columns] = act
        slope[:, columns] = (cdf + lifted * bell * 0.3989422804014327).astype(bf16)
        part = dot(act, w_down[columns, :])
        if index == 0:
            dropped[...] = part
        else:
            dropped[...] += part
    for index in range(2):
        where = pl.ds(index * half, half)
        normed = hat_one[where, :] * gain_one[...] + shift_one[...]
        hat, scale = norm(normed + dropped[where, :] + b_down[...])
        hat_two[where, :] = hat
        scale_two[where, :] = scale
        hidden_out[where, :] = (hat * gain_two[...] + shift_two[...]).astype(bf16)


def forward(pieces, weights):
    seq = pieces[0].shape[0] - 16
    rows = PIECES * seq
    (
        mask_vector,
        replace_vector,
        w_query,
        b_query,
        w_key,
        w_value,
        b_value,
        w_out,
        b_out,
        gain_one,
        shift_one,
        w_up,
        b_up,
        w_down,
        b_down,
        gain_two,
        shift_two,
    ) = weights
    specs = [VMEM] * 21
    specs[11] = specs[15] = specs[17] = HBM
    return pl.pallas_call(
        forward_kernel,
        out_shape=(
            shape((rows, D), bf16),
            shape((rows, D), bf16),
            shape((rows, D), bf16),
            shape((rows, D), bf16),
            shape((rows, D), bf16),
            shape((rows, 128), bf16),
            shape((16, rows), f32),
            shape((rows, D), f32),
            shape((rows, 1), f32),
            shape((rows, D), bf16),
            shape((rows, FF), bf16),
            shape((rows, FF), bf16),
            shape((rows, D), f32),
            shape((rows, 1), f32),
            shape((rows, D), bf16),
            shape((rows, 16), f32),
        ),
        in_specs=specs,
        out_specs=(VMEM,) * 16,
        scratch_shapes=[
            pltpu.VMEM((rows, D), f32),
            pltpu.VMEM((D, rows), bf16),
            pltpu.VMEM((D, rows), bf16),
            pltpu.VMEM((rows, D), f32),
            pltpu.VMEM((D, D), bf16),
            pltpu.VMEM((D, FF), bf16),
            pltpu.VMEM((FF, D), bf16),
            pltpu.SemaphoreType.DMA((3,)),
        ],
        compiler_params=pltpu.CompilerParams(vmem_limit_bytes=60 * MIB),
        name="forward_layer",
    )(
        *pieces,
        mask_vector,
        replace_vector,
        w_query,
        b_query,
        w_key,
        w_value,
        b_value,
        w_out,
        b_out,
        gain_one,
        shift_one,
        w_up,
        b_up,
        w_down,
        b_down,
        gain_two,
        shift_two,
    )


def sums(values):
    return jnp.sum(values, axis=0, keepdims=True)


def down_kernel(
    place,
    piece0,
    piece1,
    piece2,
    piece3,
    hat_two,
    scale_two,
    gain_two,
    active,
    grad_z_two,
    grad_dropped,
    sent,
    kept,
    vectors,
    grad_t,
):
    seq = piece0.shape[0]
    core = place[0]
    totals = [jnp.zeros((1, D), f32)] * 3
    for index, piece in enumerate((piece0, piece1, piece2, piece3)):
        where = pl.ds(index * seq, seq)
        grad = piece[...].astype(f32)
        hat = hat_two[where, :]
        grad_z = norm_back(grad, hat, scale_two[where, :], gain_two[...])
        low = grad_z.astype(bf16)
        grad_z_two[where, :] = grad_z
        grad_dropped[where, :] = low
        terms = (grad * hat, grad, low.astype(f32))
        totals = [total + sums(term) for total, term in zip(totals, terms)]
    for index in range(3):
        vectors[pl.ds(index, 1), :] = totals[index]
    block = D // PIECES
    turned = grad_dropped[...].T
    grad_t[...] = turned
    order = [1 - core, 3 - core, core, 2 + core]
    left_side = jnp.concatenate(
        [grad_t[pl.ds(pl.multiple_of(index * block, block), block), :] for index in order], axis=0
    )
    half = block // 2
    for pair in range(4):
        part = dot(left_side, active[:, pl.ds(pair * D, D)]).astype(bf16)
        for dp in range(2):
            for y in range(2):
                for ab in range(2):
                    low = y * block + ab * half
                    columns = slice(dp * 384, dp * 384 + 384)
                    sent[y, ab, pair * 2 + dp] = part[low : low + half, columns]
                    low += 2 * block
                    kept[y, ab, pair * 2 + dp] = part[low : low + half, columns]


TILES = (2, 2, 8, 96, 384)


def down_back(place, pieces, hat_two, scale_two, gain_two, active):
    rows = PIECES * pieces[0].shape[0]
    return pl.pallas_call(
        down_kernel,
        out_shape=(
            shape((rows, D), f32),
            shape((rows, D), bf16),
            shape(TILES, bf16),
            shape(TILES, bf16),
            shape((8, D), f32),
        ),
        in_specs=[SMEM] + [VMEM] * 8,
        out_specs=(VMEM,) * 5,
        scratch_shapes=[pltpu.VMEM((D, rows), bf16)],
        compiler_params=pltpu.CompilerParams(vmem_limit_bytes=60 * MIB),
        name="down_back",
    )(place, *pieces, hat_two, scale_two, gain_two, active)


def up_kernel(
    place, grad_dropped, w_down, slope, normed_low, grad_lifted, sent, kept, grad_b_up, normed_t
):
    core = place[0]
    normed_t[...] = normed_low[...].T
    block = FF // PIECES
    for index, which in enumerate([1 - core, 3 - core, core, 2 + core]):
        columns = pl.ds(pl.multiple_of(which * block, block), block)
        grad = dot_right_t(grad_dropped[...], w_down[columns, :])
        grad = (grad * slope[:, columns].astype(f32)).astype(bf16)
        grad_lifted[:, columns] = grad
        grad_b_up[:, columns] = sums(grad.astype(f32))
        part = dot(normed_t[...], grad).astype(bf16)
        target = sent if index < 2 else kept
        for dp in range(8):
            for ab in range(2):
                target[index % 2, ab, dp] = part[dp * 96 : dp * 96 + 96, ab * 384 : ab * 384 + 384]


def up_back(place, grad_dropped, w_down, slope, normed_low):
    rows = grad_dropped.shape[0]
    return pl.pallas_call(
        up_kernel,
        out_shape=(
            shape((rows, FF), bf16),
            shape(TILES, bf16),
            shape(TILES, bf16),
            shape((1, FF), f32),
        ),
        in_specs=[SMEM] + [VMEM] * 4,
        out_specs=(VMEM,) * 4,
        scratch_shapes=[pltpu.VMEM((D, rows), bf16)],
        compiler_params=pltpu.CompilerParams(vmem_limit_bytes=60 * MIB),
        name="up_back",
    )(place, grad_dropped, w_down, slope, normed_low)


def middle_kernel(
    grad_z_two,
    grad_lifted,
    w_up,
    hat_one,
    scale_one,
    gain_one,
    w_out,
    context,
    grad_z_one,
    grad_branch,
    grad_attended,
    delta,
    vectors,
):
    rows = grad_z_two.shape[0]
    half = rows // 2
    totals = [jnp.zeros((1, D), f32)] * 3
    head = lax.broadcasted_iota(jnp.int32, (16, D), 0)
    feature = lax.broadcasted_iota(jnp.int32, (16, D), 1)
    heads = (feature // HEAD_SIZE == head).astype(bf16)
    for index in range(2):
        where = pl.ds(index * half, half)
        grad = grad_z_two[where, :] + dot_right_t(grad_lifted[where, :], w_up[...])
        hat = hat_one[where, :]
        grad_z = norm_back(grad, hat, scale_one[where, :], gain_one[...])
        low = grad_z.astype(bf16)
        grad_z_one[where, :] = grad_z
        grad_branch[where, :] = low
        terms = (grad * hat, grad, low.astype(f32))
        totals = [total + sums(term) for total, term in zip(totals, terms)]
        attended = dot_right_t(low, w_out[...])
        grad_attended[where, :] = attended.astype(bf16)
        products = attended * context[where, :].astype(f32)
        high = products.astype(bf16)
        rest = (products - high.astype(f32)).astype(bf16)
        delta[:, where] = dot_right_t(heads, high) + dot_right_t(heads, rest)
    for index in range(3):
        vectors[pl.ds(index, 1), :] = totals[index]


def middle_back(grad_z_two, grad_lifted, w_up, hat_one, scale_one, gain_one, w_out, context):
    rows = grad_z_two.shape[0]
    return pl.pallas_call(
        middle_kernel,
        out_shape=(
            shape((rows, D), f32),
            shape((rows, D), bf16),
            shape((rows, D), bf16),
            shape((16, rows), f32),
            shape((8, D), f32),
        ),
        in_specs=[VMEM] * 8,
        out_specs=(VMEM,) * 5,
        compiler_params=pltpu.CompilerParams(vmem_limit_bytes=60 * MIB),
        name="middle_back",
    )(grad_z_two, grad_lifted, w_up, hat_one, scale_one, gain_one, w_out, context)


def attention_kernel(
    first,
    pairs,
    queries,
    keyed,
    valued,
    key_bias,
    stats,
    grad_attended,
    delta,
    grad_q,
    grad_k,
    grad_v,
):
    rows = queries.shape[0]
    ones_lane = (lax.broadcasted_iota(jnp.int32, (rows, 128), 1) == 0).astype(bf16)

    def pair_step(index, carry):
        pair = first + index
        columns = pl.ds(pl.multiple_of(pair * 128, 128), 128)
        out_columns = pl.ds(pl.multiple_of(index * 128, 128), 128)
        query_pair = queries[:, columns]
        query_wide = jnp.concatenate([query_pair, ones_lane], axis=1)
        key_pair = keyed[:, columns]
        key_pair_t = key_pair.T
        value_pair = valued[:, columns]
        grad_pair = grad_attended[:, columns]
        found = []
        for which in range(2):
            mine = lane_half(rows, which)
            nothing = jnp.zeros_like(key_pair)
            key_head = jnp.concatenate([jnp.where(mine, key_pair, nothing), key_bias[...]], axis=1)
            scores = dot_right_t(key_head, query_wide)
            here = pl.ds(pair * 2 + which, 1)
            weights = jnp.exp2(scores - stats[here, :])
            grad_weights = dot_right_t(jnp.where(mine, value_pair, nothing), grad_pair)
            grad_raw = (weights * (grad_weights - delta[here, :])).astype(bf16)
            grad_v_pair = dot(weights.astype(bf16), grad_pair)
            grad_k_pair = dot(grad_raw, query_pair)
            head_rows = slice(which * HEAD_SIZE, which * HEAD_SIZE + HEAD_SIZE)
            grad_q_t = dot(key_pair_t[head_rows, :], grad_raw)
            found.append((grad_q_t, grad_k_pair, grad_v_pair))
        low = lane_half(rows, 0)
        grad_q_t = jnp.concatenate([found[0][0], found[1][0]], axis=0) * HEAD_SIZE ** (-0.5)
        grad_q[:, out_columns] = grad_q_t.T.astype(bf16)
        grad_k_pair = jnp.where(low, found[0][1], found[1][1]) * (1.0 / log_two_e)
        grad_k[:, out_columns] = grad_k_pair.astype(bf16)
        grad_v[:, out_columns] = jnp.where(low, found[0][2], found[1][2]).astype(bf16)
        return carry

    lax.fori_loop(0, pairs, pair_step, 0)


def attention_back(
    first, pairs, queries, keyed, valued, key_bias, stats, grad_attended, delta
):
    rows = queries.shape[0]
    result = shape((rows, pairs * 2 * HEAD_SIZE), bf16)

    def kernel(*refs):
        attention_kernel(first, pairs, *refs)

    return pl.pallas_call(
        kernel,
        out_shape=(result, result, result),
        in_specs=[VMEM] * 7,
        out_specs=(VMEM,) * 3,
        compiler_params=pltpu.CompilerParams(vmem_limit_bytes=60 * MIB),
        name="attention_back",
    )(queries, keyed, valued, key_bias, stats, grad_attended, delta)


def weights_kernel(parts, place, *refs):
    core = place[0]
    grads = [refs[index * parts : (index + 1) * parts] for index in range(3)]
    grad_branch, entries, context, sent, kept, vectors, wide_a, wide_b, wide_c, left_e, left_c = (
        refs[3 * parts :]
    )
    grad_q, grad_k, grad_v = (
        jnp.concatenate([part[...] for part in group], axis=1) for group in grads
    )
    vectors[0:1, :] = sums(grad_q.astype(f32))
    vectors[1:2, :] = sums(grad_v.astype(f32))
    left_e[...] = entries[...].T
    left_c[...] = context[...].T
    rows = entries.shape[0]
    block = D // PIECES
    branch = grad_branch[...]
    nothing = jnp.zeros((rows, block), bf16)
    for index in range(PIECES):
        low = index * block
        wide = slice(index * 2 * block, (index + 1) * 2 * block)
        wide_a[:, wide] = jnp.concatenate(
            [grad_q[:, low : low + block], grad_k[:, low : low + block]], axis=1
        )
        wide_b[:, wide] = jnp.concatenate([grad_v[:, low : low + block], nothing], axis=1)
        wide_c[:, wide] = jnp.concatenate([nothing, branch[:, low : low + block]], axis=1)
    for index, which in enumerate([1 - core, 3 - core, core, 2 + core]):
        columns = pl.ds(pl.multiple_of(which * 2 * block, 2 * block), 2 * block)
        target = sent if index < 2 else kept
        part_a = dot(left_e[...], wide_a[:, columns]).astype(bf16)
        part_b = dot(left_e[...], wide_b[:, columns]) + dot(left_c[...], wide_c[:, columns])
        part_b = part_b.astype(bf16)
        for dp in range(8):
            target[index % 2, 0, dp] = part_a[dp * 96 : dp * 96 + 96, :]
            target[index % 2, 1, dp] = part_b[dp * 96 : dp * 96 + 96, :]


def weights_back(place, grad_q, grad_k, grad_v, grad_branch, entries, context):
    rows = entries.shape[0]
    parts = len(grad_q)

    def kernel(*refs):
        weights_kernel(parts, *refs)

    return pl.pallas_call(
        kernel,
        out_shape=(shape(TILES, bf16), shape(TILES, bf16), shape((8, D), f32)),
        in_specs=[SMEM] + [VMEM] * (3 * parts + 3),
        out_specs=(VMEM,) * 3,
        scratch_shapes=[pltpu.VMEM((rows, 2 * D), bf16)] * 3 + [pltpu.VMEM((D, rows), bf16)] * 2,
        compiler_params=pltpu.CompilerParams(vmem_limit_bytes=60 * MIB),
        name="weights_back",
    )(place, *grad_q, *grad_k, *grad_v, grad_branch, entries, context)


def start_kernel(parts, *refs):
    grads = [refs[index * parts : (index + 1) * parts] for index in range(3)]
    w_query, w_key, w_value, grad_z_one, flags, piece0, piece1, piece2, piece3, vectors = refs[
        3 * parts :
    ]
    pieces = (piece0, piece1, piece2, piece3)
    seq = piece0.shape[0]
    totals = [jnp.zeros((1, D), f32)] * 2
    for step in range(2):
        where = pl.ds(step * 2 * seq, 2 * seq)
        grad = grad_z_one[where, :]
        for group, weight in zip(grads, (w_query, w_key, w_value)):
            value = jnp.concatenate([part[where, :] for part in group], axis=1)
            grad = grad + dot_right_t(value, weight[...])
        masked = flags[where, 1:2]
        replaced = flags[where, 2:3]
        terms = (grad * masked, grad * replaced)
        totals = [total + sums(term) for total, term in zip(totals, terms)]
        low = jnp.where(masked > 0, 0.0, grad).astype(bf16)
        pieces[2 * step][...] = low[:seq, :]
        pieces[2 * step + 1][...] = low[seq:, :]
    for index in range(2):
        vectors[pl.ds(index, 1), :] = totals[index]


def start_back(grad_q, grad_k, grad_v, w_query, w_key, w_value, grad_z_one, flags):
    rows = grad_z_one.shape[0]
    parts = len(grad_q)

    def kernel(*refs):
        start_kernel(parts, *refs)

    return pl.pallas_call(
        kernel,
        out_shape=(shape((rows // PIECES, D), bf16),) * PIECES + (shape((8, D), f32),),
        in_specs=[VMEM] * (3 * parts + 5),
        out_specs=(VMEM,) * 5,
        compiler_params=pltpu.CompilerParams(vmem_limit_bytes=60 * MIB),
        name="start_back",
    )(*grad_q, *grad_k, *grad_v, w_query, w_key, w_value, grad_z_one, flags)


def swap(value, axis, bit):
    size = lax.axis_size(axis)
    return lax.ppermute(value, axis, [(i, i ^ bit) for i in range(size)])


def pick(value, axis, index):
    return lax.dynamic_index_in_dim(value, index, axis, keepdims=False)


def total(terms):
    result = terms[0].astype(f32)
    for term in terms[1:]:
        result = result + term.astype(f32)
    return result


def reduce_tiles(sent, kept):
    blk = lax.axis_index("blk")
    fine = lax.axis_size("dp") // 8
    coarse = lax.axis_index("dp") // fine
    y = blk // 2
    bit0 = coarse % 2
    bit1 = (coarse // 2) % 2
    bit2 = coarse // 4
    split = (2, 2, 2, 2, 2) + TILES[3:]
    terms = [kept.reshape(split), swap(sent, "blk", 1).reshape(split)]
    terms_a = [t[:, 0] for t in terms]
    terms_b = [t[:, 1] for t in terms]
    send_a = total([pick(t, 3, 1 - bit0) for t in terms_a]).astype(bf16)
    send_b = total([pick(t, 0, 1 - y) for t in terms_b]).astype(bf16)
    got_a = swap(send_a, "dp", fine)
    got_b = swap(send_b, "blk", 2)
    terms_a = [pick(t, 3, bit0) for t in terms_a] + [got_a]
    terms_b = [pick(t, 0, y) for t in terms_b] + [got_b]
    send_a = total([pick(t, 0, 1 - y) for t in terms_a]).astype(bf16)
    send_b = total([pick(t, 2, 1 - bit0) for t in terms_b]).astype(bf16)
    got_a = swap(send_a, "blk", 2)
    got_b = swap(send_b, "dp", fine)
    terms_a = [pick(t, 0, y) for t in terms_a] + [got_a]
    terms_b = [pick(t, 2, bit0) for t in terms_b] + [got_b]
    send = jnp.stack(
        [total([pick(t, 1, 1 - bit1) for t in group]) for group in (terms_a, terms_b)]
    ).astype(bf16)
    got = swap(send, "dp", 2 * fine)
    terms_a = [pick(t, 1, bit1) for t in terms_a] + [got[0]]
    terms_b = [pick(t, 1, bit1) for t in terms_b] + [got[1]]
    send = jnp.stack(
        [total([pick(t, 0, 1 - bit2) for t in group]) for group in (terms_a, terms_b)]
    ).astype(bf16)
    got = swap(send, "dp", 4 * fine)
    part_a = total([pick(t, 0, bit2) for t in terms_a] + [got[0]])
    part_b = total([pick(t, 0, bit2) for t in terms_b] + [got[1]])
    return part_a, part_b


def finish(tile, axis):
    size = lax.axis_size("dp")
    fine = size // 8
    if fine == 1:
        return tile
    groups = [[index * fine + item for item in range(fine)] for index in range(8)]
    return lax.psum_scatter(
        tile, "dp", scatter_dimension=axis, axis_index_groups=groups, tiled=True
    )


def sum_vectors(value):
    for bit in (1, 2):
        value = value + swap(value, "blk", bit)
    bit = 1
    while bit < lax.axis_size("dp"):
        value = value + swap(value, "dp", bit)
        bit *= 2
    return value


def spread_documents(value):
    blk = lax.axis_index("blk")
    own = pick(value, 0, blk)
    return [own] + [swap(pick(value, 0, blk ^ step), "blk", step) for step in range(1, PIECES)]


def gather_documents(pieces):
    blk = lax.axis_index("blk")
    back = [pieces[0]] + [swap(pieces[step], "blk", step) for step in range(1, PIECES)]
    low = blk % 2 == 1
    high = blk // 2 == 1
    back = [jnp.where(low, back[index ^ 1], back[index]) for index in range(PIECES)]
    back = [jnp.where(high, back[index ^ 2], back[index]) for index in range(PIECES)]
    return jnp.stack(back)


def local(
    hidden_in,
    pad_mask,
    masked_flag,
    replaced_flag,
    mask_vector,
    replace_vector,
    w_query,
    b_query,
    w_key,
    w_value,
    b_value,
    w_out,
    b_out,
    gain_one,
    shift_one,
    w_up,
    b_up,
    w_down,
    b_down,
    gain_two,
    shift_two,
    out_grad,
):
    doc_count, seq_rows = pad_mask.shape
    row = lambda vector: vector.reshape(1, -1)
    place = (lax.axis_index("blk") % 2).astype(jnp.int32).reshape(1)
    flags = jnp.stack([pad_mask, masked_flag, replaced_flag], axis=1).astype(bf16)
    flags = jnp.pad(flags, ((0, 0), (0, 13), (0, D - seq_rows)))
    pieces = spread_documents(jnp.concatenate([hidden_in, flags], axis=1))
    grad_pieces = spread_documents(out_grad)
    (
        entries,
        queries,
        keyed,
        valued,
        context,
        key_bias,
        stats,
        hat_one,
        scale_one,
        normed_low,
        active,
        slope,
        hat_two,
        scale_two,
        hidden_out,
        columns,
    ) = forward(
        pieces,
        (
            row(mask_vector),
            row(replace_vector),
            w_query,
            row(b_query),
            w_key,
            w_value,
            row(b_value),
            w_out,
            row(b_out),
            row(gain_one),
            row(shift_one),
            w_up,
            row(b_up),
            w_down,
            row(b_down),
            row(gain_two),
            row(shift_two),
        ),
    )
    grad_z_two, grad_dropped, sent, kept, vectors_two = down_back(
        place, grad_pieces, hat_two, scale_two, row(gain_two), active
    )
    down_a, down_b = reduce_tiles(sent, kept)
    hidden_out = gather_documents(
        [hidden_out[index * seq_rows : (index + 1) * seq_rows] for index in range(PIECES)]
    )
    grad_lifted, sent, kept, grad_b_up = up_back(place, grad_dropped, w_down, slope, normed_low)
    up_a, up_b = reduce_tiles(sent, kept)
    grad_z_one, grad_branch, grad_attended, delta, vectors_one = middle_back(
        grad_z_two, grad_lifted, w_up, hat_one, scale_one, row(gain_one), w_out, context
    )
    early = sum_vectors(
        jnp.concatenate([vectors_two[:3], vectors_one[:3], grad_b_up.reshape(-1, D)], axis=0)
    )
    grads = [
        attention_back(
            first, 2, queries, keyed, valued, key_bias, stats, grad_attended, delta
        )
        for first in (0, 2, 4)
    ]
    grad_q, grad_k, grad_v = zip(*grads)
    sent, kept, vectors_qv = weights_back(
        place, grad_q, grad_k, grad_v, grad_branch, entries, context
    )
    pair_a, pair_b = reduce_tiles(sent, kept)
    *grad_in, vectors_start = start_back(
        grad_q, grad_k, grad_v, w_query, w_key, w_value, grad_z_one, columns
    )
    grad_in = gather_documents(grad_in)
    late = sum_vectors(jnp.concatenate([vectors_start[:2], vectors_qv[:2]], axis=0))
    block = D // PIECES
    grad_w_down = finish(jnp.concatenate([down_a, down_b], axis=0).T, 0)
    grad_w_up = finish(jnp.concatenate([up_a, up_b], axis=1), 0)
    pair_a = finish(pair_a, 0)
    pair_b = finish(pair_b, 0)
    return (
        hidden_out,
        grad_in,
        late[0],
        late[1],
        pair_a[:, :block],
        late[2],
        pair_a[:, block:],
        pair_b[:, :block],
        late[3],
        pair_b[:, block:],
        early[5],
        early[3],
        early[4],
        grad_w_up,
        early[6:].reshape(-1),
        grad_w_down,
        early[2],
        early[0],
        early[1],
    )


def solution(mesh):
    replicated = (P(),) * 17
    placed = (P("dp", "blk", None),) + (P("dp", "blk"),) * 3 + replicated
    placed = placed + (P("dp", "blk", None),)
    tiles = P("dp", "blk")
    rows = P("dp", "blk", None)
    return jax.shard_map(
        local,
        mesh=mesh,
        in_specs=placed,
        out_specs=(
            rows,
            rows,
            P(),
            P(),
            tiles,
            P(),
            tiles,
            tiles,
            P(),
            tiles,
            P(),
            P(),
            P(),
            tiles,
            P(),
            tiles,
            P(),
            P(),
            P(),
        ),
        check_vma=False,
    )
```

time: 987 us -> 251 us (0.25)
  waiting for transfers between devices: 630 us -> 73.7 us
  matrix products: 121 us -> 0 us
  local copies, waits for them, and re-layouts: 144 us -> 26.8 us
  Pallas kernels: 0 us -> 90 us
  blocking collectives: 47.4 us -> 0 us
  starting transfers between devices: 0.63 us -> 42.5 us
  between operations: 15.5 us -> 1.5 us
    reduce_scatter x6 -> x0, waiting for transfers between devices: 574 us -> none  [the longest x1 142 us: local(): lax.psum_scatter(down_tiles, ('dp', 'blk'), scatter_dimension=0, tiled=True)]
    dot_general x24 -> x0, matrix products: 121 us -> none  [the longest x6 30.9 us: matmul(): return jnp.dot(left_side, right_side, preferred_element_type=jnp.float32)]
    pallas_call x0 -> x9, Pallas kernels: none -> 90 us  [the longest x1 26.1 us: forward(): pl.pallas_call(forward_kernel, out_shape=(shape((rows, D), bf16), shape((...]
    ppermute x0 -> x43, waiting for transfers between devices: none -> 73.7 us  [swap(): return lax.ppermute(value, axis, [(i, i ^ bit) for i in range(size)])]
    unnamed x128 -> x65, local copies, waits for them, and re-layouts: 74.7 us -> 2.36 us
    ppermute x0 -> x43, starting transfers between devices: none -> 42.5 us  [swap(): return lax.ppermute(value, axis, [(i, i ^ bit) for i in range(size)])]
    psum x1 -> x0, blocking collectives: 41.3 us -> none  [local(): lax.psum((grad_mask_vector, grad_replace_vector, grad_b_query, grad_b_val...]
    all_gather x2 -> x0, waiting for transfers between devices: 37.1 us -> none  [the longest x1 20.9 us: local(): key_piece = lax.all_gather(keyed, 'blk', axis=1, tiled=True)]
  transfers between devices with their start and end apart: 10 -> 43, of which waited for: 8 -> 19; matrix products, arithmetic and copies ran while one was open for 17% -> 13% of each run, Pallas kernels for 0% -> 17%
where the time goes in v1:
time: 251 us; the launch traced here: 247 us
  Pallas kernels  90 us (36%)
  waiting for transfers between devices  73.7 us (29%)
  starting transfers between devices  42.5 us (17%)
  local copies, waits for them, and re-layouts  26.8 us (11%)
  other arithmetic  12.5 us (5%)
    ppermute x43, waiting for transfers between devices, swap(): return lax.ppermute(value, axis, [(i, i ^ bit) for i in range(size)])  73.7 us
    ppermute x43, starting transfers between devices, swap(): return lax.ppermute(value, axis, [(i, i ^ bit) for i in range(size)])  42.5 us
    pallas_call x1, Pallas kernels, forward(): pl.pallas_call(forward_kernel, out_shape=(shape((rows, D), bf16), shape((...  26.1 us
    pallas_call x3, Pallas kernels, attention_back(): pl.pallas_call(kernel, out_shape=(result, result, result), in_specs=[VMEM...  17.5 us
    pallas_call x1, Pallas kernels, up_back(): pl.pallas_call(up_kernel, out_shape=(shape((rows, FF), bf16), shape(TILES...  10.8 us
    pallas_call x1, Pallas kernels, middle_back(): pl.pallas_call(middle_kernel, out_shape=(shape((rows, D), f32), shape((ro...  10.6 us
    slice x6, local copies, waits for them, and re-layouts, reduce_tiles(): terms_a = [t[:, 0] for t in terms]  9.73 us
    pallas_call x1, Pallas kernels, down_back(): pl.pallas_call(down_kernel, out_shape=(shape((rows, D), f32), shape((rows...  9.51 us
  transfers between devices with their start and end apart: 43, of which 19 were waited for; matrix products, arithmetic and copies ran while one was open for 13% of the time, Pallas kernels for 17%

profile of v1, /device:TPU:0, one launch (start us, length us, event | category | flops | bytes accessed | tf_op | source)
XLA Modules:
  0.0 247.1 jit_solution(2217190360713801510)
XLA Ops:
  4.7 2.6 %collective-permute-start.1 = (bf16[144,768]{1,0:T(8,128)(2,1)S(1)}, bf16[144,768]{1,0:T(8,128)(2,1)S(1)}, u32[]{:S(2)}, u32[]{:S(2)}) collective-permute-start(bf16[144,768]{1,0:T(8,128)(2,1)S(1)} %get-tuple-element.140), channel_id=1, source_target_pairs={{0,2},{1,3},{2,0},{3,1},{4,6},{5,7},{6,4},{7,5},{8,10},{9,11},{10,... | collective-permute-start | bytes 663560 | tf_op jit(solution)/shard_map/ppermute | solution.py:632
  18.5 26.1 %forward_layer.1 = (bf16[512,768]{1,0:T(8,128)(2,1)}, bf16[512,768]{1,0:T(8,128)(2,1)}, bf16[512,768]{1,0:T(8,128)(2,1)}, bf16[512,768]{1,0:T(8,128)(2,1)}, bf16...) custom-call(bf16[144,768]{1,0:T(8,128)(2,1)} %get-tuple-element.142., ...), custom_call_target="tpu_custom_call" | custom-call | tf_op jit(solution)/shard_map/forward_layer/pallas_call | solution.py:232
  45.4 9.5 %down_back.1 = (f32[512,768]{1,0:T(8,128)}, bf16[512,768]{1,0:T(8,128)(2,1)}, bf16[2,2,8,96,384]{4,3,2,1,0:T(8,128)(2,1)}, bf16[2,2,8,96,384]{4,3,2,1,0:T(8,128)(2,1)}, f32[8,768]{1,0:T(8,128)}) custom-call(s32[1]{0:T(128)} %bitcast.12.place.refs_0_, bf16[128,768]{1,0:T(8,128)(2,1)} %get-tuple-element.149.piece0, bf16[128,768]{1,0:T(8,128)(2,1)} %copy-done.11, ...), custom_call_target="tpu_custom_call" | custom-call | tf_op jit(solution)/shard_map/down_back/pallas_call | solution.py:349
  54.9 10.8 %up_back.1 = (bf16[512,3072]{1,0:T(8,128)(2,1)}, bf16[2,2,8,96,384]{4,3,2,1,0:T(8,128)(2,1)}, bf16[2,2,8,96,384]{4,3,2,1,0:T(8,128)(2,1)}, f32[1,3072]{1,0:T(1,128)}) custom-call(s32[1]{0:T(128)} %bitcast.12.place.refs_0_, bf16[512,768]{1,0:T(8,128)(2,1)} %get-tuple-element.76.grad_dropped, bf16[3072,768]{1,0:T(8,128)(2,1)} %w_down.1, ...), custom_call_target="tpu_custom_call" | custom-call | tf_op jit(solution)/shard_map/up_back/pallas_call | solution.py:387
  65.8 10.6 %middle_back.1 = (f32[512,768]{1,0:T(8,128)}, bf16[512,768]{1,0:T(8,128)(2,1)}, bf16[512,768]{1,0:T(8,128)(2,1)}, f32[16,512]{1,0:T(8,128)}, f32[8,768]{1,0:T(8,128)}) custom-call(f32[512,768]{1,0:T(8,128)} %get-tuple-element.75.grad_z_two, bf16[512,3072]{1,0:T(8,128)(2,1)} %get-tuple-element.79.grad_lifted, bf16[768,3072]{1,0:T(8,128)(2,1)} %w_up.1, ...), custom_call_target="tpu_custom_call" | custom-call | tf_op jit(solution)/shard_map/middle_back/pallas_call | solution.py:446
  76.3 5.8 %attention_back.5 = (bf16[512,256]{1,0:T(8,128)(2,1)}, bf16[512,256]{1,0:T(8,128)(2,1)}, bf16[512,256]{1,0:T(8,128)(2,1)}) custom-call(bf16[512,768]{1,0:T(8,128)(2,1)} %get-tuple-element.67.refs_0_, bf16[512,768]{1,0:T(8,128)(2,1)} %get-tuple-element.68.refs_1_, bf16[512,768]{1,0:T(8,128)(2,1)} %get-tuple-element.69.refs_2_, ...), custom_call_target="tpu_custom_call" | custom-call | tf_op jit(solution)/shard_map/attention_back/pallas_call | solution.py:524
  82.1 5.8 %attention_back.4 = (bf16[512,256]{1,0:T(8,128)(2,1)}, bf16[512,256]{1,0:T(8,128)(2,1)}, bf16[512,256]{1,0:T(8,128)(2,1)}) custom-call(bf16[512,768]{1,0:T(8,128)(2,1)} %get-tuple-element.67.refs_0_, bf16[512,768]{1,0:T(8,128)(2,1)} %get-tuple-element.68.refs_1_, bf16[512,768]{1,0:T(8,128)(2,1)} %get-tuple-element.69.refs_2_, ...), custom_call_target="tpu_custom_call" | custom-call | tf_op jit(solution)/shard_map/attention_back/pallas_call | solution.py:524
  87.9 5.9 %attention_back.3 = (bf16[512,256]{1,0:T(8,128)(2,1)}, bf16[512,256]{1,0:T(8,128)(2,1)}, bf16[512,256]{1,0:T(8,128)(2,1)}) custom-call(bf16[512,768]{1,0:T(8,128)(2,1)} %get-tuple-element.67.refs_0_, bf16[512,768]{1,0:T(8,128)(2,1)} %get-tuple-element.68.refs_1_, bf16[512,768]{1,0:T(8,128)(2,1)} %get-tuple-element.69.refs_2_, ...), custom_call_target="tpu_custom_call" | custom-call | tf_op jit(solution)/shard_map/attention_back/pallas_call | solution.py:524
  95.7 9.3 %weights_back.1 = (bf16[2,2,8,96,384]{4,3,2,1,0:T(8,128)(2,1)}, bf16[2,2,8,96,384]{4,3,2,1,0:T(8,128)(2,1)}, f32[8,768]{1,0:T(8,128)}) custom-call(s32[1]{0:T(128)} %bitcast.12.place.refs_0_, bf16[512,256]{1,0:T(8,128)(2,1)} %get-tuple-element.85.refs_0_.refs_1_, bf16[512,256]{1,0:T(8,128)(2,1)} %get-tuple-element.86.refs_1_.refs_2_, ...), custom_call_target="tpu_custom_call" | custom-call | tf_op jit(solution)/shard_map/weights_back/pallas_call | solution.py:577
  105.7 6.2 %start_back.1 = (bf16[128,768]{1,0:T(8,128)(2,1)}, bf16[128,768]{1,0:T(8,128)(2,1)}, bf16[128,768]{1,0:T(8,128)(2,1)}, bf16[128,768]{1,0:T(8,128)(2,1)}, f32[8,768]{1,0:T(8,128)}) custom-call(bf16[512,256]{1,0:T(8,128)(2,1)} %get-tuple-element.85.refs_0_.refs_1_, bf16[512,256]{1,0:T(8,128)(2,1)} %get-tuple-element.86.refs_1_.refs_2_, ...), custom_call_target="tpu_custom_call" | custom-call | tf_op jit(solution)/shard_map/start_back/pallas_call | solution.py:620
  115.9 3.0 %collective-permute-done.13 = f32[4,768]{1,0:T(4,128)S(1)} collective-permute-done((f32[4,768]{1,0:T(4,128)S(1)}, f32[4,768]{1,0:T(4,128)S(1)}, u32[]{:S(2)}, u32[]{:S(2)}) %collective-permute-start.13) | collective-permute-done | bytes 12320 | tf_op jit(solution)/shard_map/ppermute | solution.py:632
  127.5 2.7 %collective-permute-start.16 = (f32[4,768]{1,0:T(4,128)S(1)}, f32[4,768]{1,0:T(4,128)S(1)}, u32[]{:S(2)}, u32[]{:S(2)}) collective-permute-start(f32[4,768]{1,0:T(4,128)S(1)} %add.1586), channel_id=1, source_target_pairs={{0,16},{4,20},{8,24},{12,28},{16,0},{20,4},{24,8},{28,12},{1,17},{... | collective-permute-start | bytes 36872 | tf_op jit(solution)/shard_map/ppermute | solution.py:632
  133.4 2.5 %collective-permute-done.28 = f32[10,768]{1,0:T(8,128)S(1)} collective-permute-done((f32[10,768]{1,0:T(8,128)S(1)}, f32[10,768]{1,0:T(8,128)S(1)}, u32[]{:S(2)}, u32[]{:S(2)}) %collective-permute-start.28) | collective-permute-done | bytes 30752 | tf_op jit(solution)/shard_map/ppermute | solution.py:632
  143.9 2.2 collective-permute-done.9
  146.9 2.8 %collective-permute-done.3 = bf16[128,768]{1,0:T(8,128)(2,1)} collective-permute-done((bf16[128,768]{1,0:T(8,128)(2,1)}, bf16[128,768]{1,0:T(8,128)(2,1)}, u32[]{:S(2)}, u32[]{:S(2)}) %collective-permute-start.3) | collective-permute-done | bytes 196640 | tf_op jit(solution)/shard_map/ppermute | solution.py:632
  168.2 6.2 %collective-permute-done.37 = bf16[2,2,2,96,384]{4,3,2,1,0:T(8,128)(2,1)S(1)} collective-permute-done((bf16[2,2,2,96,384]{4,3,2,1,0:T(8,128)(2,1)S(1)}, bf16[2,2,2,96,384]{4,3,2,1,0:T(8,128)(2,1)S(1)}, u32[]{:S(2)}, u32[]{:S(2)}) %collective-permute-start.37) | collective-permute-done | bytes 589856 | tf_op jit(solution)/shard_map/ppermute | solution.py:632
  176.7 10.3 %collective-permute-done.30 = bf16[2,2,2,96,384]{4,3,2,1,0:T(8,128)(2,1)S(1)} collective-permute-done((bf16[2,2,2,96,384]{4,3,2,1,0:T(8,128)(2,1)S(1)}, bf16[2,2,2,96,384]{4,3,2,1,0:T(8,128)(2,1)S(1)}, u32[]{:S(2)}, u32[]{:S(2)}) %collective-permute-start.30) | collective-permute-done | bytes 589856 | tf_op jit(solution)/shard_map/ppermute | solution.py:632
  189.3 10.3 %collective-permute-done.18 = bf16[2,2,2,96,384]{4,3,2,1,0:T(8,128)(2,1)S(1)} collective-permute-done((bf16[2,2,2,96,384]{4,3,2,1,0:T(8,128)(2,1)S(1)}, bf16[2,2,2,96,384]{4,3,2,1,0:T(8,128)(2,1)S(1)}, u32[]{:S(2)}, u32[]{:S(2)}) %collective-permute-start.18) | collective-permute-done | bytes 589856 | tf_op jit(solution)/shard_map/ppermute | solution.py:632
  202.2 4.9 %collective-permute-done.38 = bf16[2,2,96,384]{3,2,0,1:T(8,128)(2,1)S(1)} collective-permute-done((bf16[2,2,96,384]{3,2,0,1:T(8,128)(2,1)S(1)}, bf16[2,2,96,384]{3,2,0,1:T(8,128)(2,1)S(1)}, u32[]{:S(2)}, u32[]{:S(2)}) %collective-permute-start.38) | collective-permute-done | bytes 294944 | tf_op jit(solution)/shard_map/ppermute | solution.py:632
  209.8 3.7 %collective-permute-done.31 = bf16[2,2,96,384]{3,2,0,1:T(8,128)(2,1)S(1)} collective-permute-done((bf16[2,2,96,384]{3,2,0,1:T(8,128)(2,1)S(1)}, bf16[2,2,96,384]{3,2,0,1:T(8,128)(2,1)S(1)}, u32[]{:S(2)}, u32[]{:S(2)}) %collective-permute-start.31) | collective-permute-done | bytes 294944 | tf_op jit(solution)/shard_map/ppermute | solution.py:632
  215.0 3.5 %collective-permute-done.19 = bf16[2,2,96,384]{3,2,0,1:T(8,128)(2,1)S(1)} collective-permute-done((bf16[2,2,96,384]{3,2,0,1:T(8,128)(2,1)S(1)}, bf16[2,2,96,384]{3,2,0,1:T(8,128)(2,1)S(1)}, u32[]{:S(2)}, u32[]{:S(2)}) %collective-permute-start.19) | collective-permute-done | bytes 294944 | tf_op jit(solution)/shard_map/ppermute | solution.py:632
  222.1 8.9 %collective-permute-done.22 = bf16[2,2,96,384]{3,2,1,0:T(8,128)(2,1)S(1)} collective-permute-done((bf16[2,2,96,384]{3,2,1,0:T(8,128)(2,1)S(1)}, bf16[2,2,96,384]{3,2,1,0:T(8,128)(2,1)S(1)}, u32[]{:S(2)}, u32[]{:S(2)}) %collective-permute-start.22) | collective-permute-done | bytes 294944 | tf_op jit(solution)/shard_map/ppermute | solution.py:632
  232.3 2.3 collective-permute-start.35
  234.6 9.0 %collective-permute-done.23 = bf16[2,96,384]{2,1,0:T(8,128)(2,1)S(1)} collective-permute-done((bf16[2,96,384]{2,1,0:T(8,128)(2,1)S(1)}, bf16[2,96,384]{2,1,0:T(8,128)(2,1)S(1)}, u32[]{:S(2)}, u32[]{:S(2)}) %collective-permute-start.23) | collective-permute-done | bytes 147488 | tf_op jit(solution)/shard_map/ppermute | solution.py:632
  (229 shorter events, 80.9 us)
Async XLA Ops:
  8.0 36.6 %collective-permute-start.6 = (bf16[128,768]{1,0:T(8,128)(2,1)S(1)}, bf16[128,768]{1,0:T(8,128)(2,1)S(1)}, u32[]{:S(2)}, u32[]{:S(2)}) collective-permute-start(bf16[128,768]{1,0:T(8,128)(2,1)S(1)} %get-tuple-element.148), channel_id=1, source_target_pairs={{0,1},{1,0},{2,3},{3,2},{4,5},{5,4},{6,7},{7,6},{8,9},{9,8},{10,11... | collective-permute-start | bytes 589832 | tf_op jit(solution)/shard_map/ppermute | solution.py:632
  8.2 36.4 %collective-permute-start.7 = (bf16[128,768]{1,0:T(8,128)(2,1)S(1)}, bf16[128,768]{1,0:T(8,128)(2,1)S(1)}, u32[]{:S(2)}, u32[]{:S(2)}) collective-permute-start(bf16[128,768]{1,0:T(8,128)(2,1)S(1)} %get-tuple-element.150), channel_id=1, source_target_pairs={{0,2},{1,3},{2,0},{3,1},{4,6},{5,7},{6,4},{7,5},{8,10},{9,11},{10,... | collective-permute-start | bytes 589832 | tf_op jit(solution)/shard_map/ppermute | solution.py:632
  10.1 34.5 %collective-permute-start.8 = (bf16[128,768]{1,0:T(8,128)(2,1)S(1)}, bf16[128,768]{1,0:T(8,128)(2,1)S(1)}, u32[]{:S(2)}, u32[]{:S(2)}) collective-permute-start(bf16[128,768]{1,0:T(8,128)(2,1)S(1)} %get-tuple-element.147), channel_id=1, source_target_pairs={{0,3},{1,2},{2,1},{3,0},{4,7},{5,6},{6,5},{7,4},{8,11},{9,10},{10,... | collective-permute-start | bytes 589832 | tf_op jit(solution)/shard_map/ppermute | solution.py:632
  93.8 62.1 %collective-permute-start.36 = (bf16[2,2,8,96,384]{4,3,2,1,0:T(8,128)(2,1)}, bf16[2,2,8,96,384]{4,3,2,1,0:T(8,128)(2,1)}, u32[]{:S(2)}, u32[]{:S(2)}) collective-permute-start(bf16[2,2,8,96,384]{4,3,2,1,0:T(8,128)(2,1)} %get-tuple-element.112), channel_id=1, source_target_pairs={{0,1},{1,0},{2,3},{3,2},{4,5},{5,4},{6,7},{7,6},{8,9},{9,8},{10,11... | collective-permute-start | bytes 7077896 | tf_op jit(solution)/shard_map/ppermute | solution.py:632
  95.4 17.6 %collective-permute-start.24 = (f32[10,768]{1,0:T(8,128)S(1)}, f32[10,768]{1,0:T(8,128)S(1)}, u32[]{:S(2)}, u32[]{:S(2)}) collective-permute-start(f32[10,768]{1,0:T(8,128)S(1)} %pad_maximum_fusion.9), channel_id=1, source_target_pairs={{0,1},{1,0},{2,3},{3,2},{4,5},{5,4},{6,7},{7,6},{8,9},{9,8},{10,11... | collective-permute-start | bytes 92168 | tf_op jit(solution)/shard_map/ppermute | solution.py:632
  122.4 38.0 %collective-permute-start.29 = (bf16[2,2,8,96,384]{4,3,2,1,0:T(8,128)(2,1)}, bf16[2,2,8,96,384]{4,3,2,1,0:T(8,128)(2,1)}, u32[]{:S(2)}, u32[]{:S(2)}) collective-permute-start(bf16[2,2,8,96,384]{4,3,2,1,0:T(8,128)(2,1)} %get-tuple-element.110), channel_id=1, source_target_pairs={{0,1},{1,0},{2,3},{3,2},{4,5},{5,4},{6,7},{7,6},{8,9},{9,8},{10,11... | collective-permute-start | bytes 7077896 | tf_op jit(solution)/shard_map/ppermute | solution.py:632
  127.5 37.3 %collective-permute-start.17 = (bf16[2,2,8,96,384]{4,3,2,1,0:T(8,128)(2,1)}, bf16[2,2,8,96,384]{4,3,2,1,0:T(8,128)(2,1)}, u32[]{:S(2)}, u32[]{:S(2)}) collective-permute-start(bf16[2,2,8,96,384]{4,3,2,1,0:T(8,128)(2,1)} %get-tuple-element.105), channel_id=1, source_target_pairs={{0,1},{1,0},{2,3},{3,2},{4,5},{5,4},{6,7},{7,6},{8,9},{9,8},{10,11... | collective-permute-start | bytes 7077896 | tf_op jit(solution)/shard_map/ppermute | solution.py:632
  158.0 16.3 %collective-permute-start.37 = (bf16[2,2,2,96,384]{4,3,2,1,0:T(8,128)(2,1)S(1)}, bf16[2,2,2,96,384]{4,3,2,1,0:T(8,128)(2,1)S(1)}, u32[]{:S(2)}, u32[]{:S(2)}) collective-permute-start(bf16[2,2,2,96,384]{4,3,2,1,0:T(8,128)(2,1)S(1)} %copy.60), channel_id=1, source_target_pairs={{0,4},{4,0},{8,12},{12,8},{16,20},{20,16},{24,28},{28,24},{1,5},{5... | collective-permute-start | bytes 1769480 | tf_op jit(solution)/shard_map/ppermute | solution.py:632
  159.2 16.3 %collective-permute-start.39 = (bf16[2,2,2,96,384]{4,3,2,1,0:T(8,128)(2,1)S(1)}, bf16[2,2,2,96,384]{4,3,2,1,0:T(8,128)(2,1)S(1)}, u32[]{:S(2)}, u32[]{:S(2)}) collective-permute-start(bf16[2,2,2,96,384]{4,3,2,1,0:T(8,128)(2,1)S(1)} %fusion.7), channel_id=1, source_target_pairs={{0,2},{1,3},{2,0},{3,1},{4,6},{5,7},{6,4},{7,5},{8,10},{9,11},{10,... | collective-permute-start | bytes 1769480 | tf_op jit(solution)/shard_map/ppermute | solution.py:632
  162.6 24.4 %collective-permute-start.30 = (bf16[2,2,2,96,384]{4,3,2,1,0:T(8,128)(2,1)S(1)}, bf16[2,2,2,96,384]{4,3,2,1,0:T(8,128)(2,1)S(1)}, u32[]{:S(2)}, u32[]{:S(2)}) collective-permute-start(bf16[2,2,2,96,384]{4,3,2,1,0:T(8,128)(2,1)S(1)} %copy.52), channel_id=1, source_target_pairs={{0,4},{4,0},{8,12},{12,8},{16,20},{20,16},{24,28},{28,24},{1,5},{5... | collective-permute-start | bytes 1769480 | tf_op jit(solution)/shard_map/ppermute | solution.py:632
  163.8 24.3 %collective-permute-start.32 = (bf16[2,2,2,96,384]{4,3,2,1,0:T(8,128)(2,1)S(1)}, bf16[2,2,2,96,384]{4,3,2,1,0:T(8,128)(2,1)S(1)}, u32[]{:S(2)}, u32[]{:S(2)}) collective-permute-start(bf16[2,2,2,96,384]{4,3,2,1,0:T(8,128)(2,1)S(1)} %fusion.5), channel_id=1, source_target_pairs={{0,2},{1,3},{2,0},{3,1},{4,6},{5,7},{6,4},{7,5},{8,10},{9,11},{10,... | collective-permute-start | bytes 1769480 | tf_op jit(solution)/shard_map/ppermute | solution.py:632
  167.0 32.6 %collective-permute-start.18 = (bf16[2,2,2,96,384]{4,3,2,1,0:T(8,128)(2,1)S(1)}, bf16[2,2,2,96,384]{4,3,2,1,0:T(8,128)(2,1)S(1)}, u32[]{:S(2)}, u32[]{:S(2)}) collective-permute-start(bf16[2,2,2,96,384]{4,3,2,1,0:T(8,128)(2,1)S(1)} %copy.44), channel_id=1, source_target_pairs={{0,4},{4,0},{8,12},{12,8},{16,20},{20,16},{24,28},{28,24},{1,5},{5... | collective-permute-start | bytes 1769480 | tf_op jit(solution)/shard_map/ppermute | solution.py:632
  174.3 26.5 %collective-permute-start.20 = (bf16[2,2,2,96,384]{4,3,2,1,0:T(8,128)(2,1)S(1)}, bf16[2,2,2,96,384]{4,3,2,1,0:T(8,128)(2,1)S(1)}, u32[]{:S(2)}, u32[]{:S(2)}) collective-permute-start(bf16[2,2,2,96,384]{4,3,2,1,0:T(8,128)(2,1)S(1)} %fusion.3), channel_id=1, source_target_pairs={{0,2},{1,3},{2,0},{3,1},{4,6},{5,7},{6,4},{7,5},{8,10},{9,11},{10,... | collective-permute-start | bytes 1769480 | tf_op jit(solution)/shard_map/ppermute | solution.py:632
  175.5 31.6 %collective-permute-start.38 = (bf16[2,2,96,384]{3,2,0,1:T(8,128)(2,1)S(1)}, bf16[2,2,96,384]{3,2,0,1:T(8,128)(2,1)S(1)}, u32[]{:S(2)}, u32[]{:S(2)}) collective-permute-start(bf16[2,2,96,384]{3,2,0,1:T(8,128)(2,1)S(1)} %fusion.9), channel_id=1, source_target_pairs={{0,2},{1,3},{2,0},{3,1},{4,6},{5,7},{6,4},{7,5},{8,10},{9,11},{10,... | collective-permute-start | bytes 884744 | tf_op jit(solution)/shard_map/ppermute | solution.py:632
  187.0 21.3 %collective-permute-start.40 = (bf16[2,2,96,384]{3,2,1,0:T(8,128)(2,1)S(1)}, bf16[2,2,96,384]{3,2,1,0:T(8,128)(2,1)S(1)}, u32[]{:S(2)}, u32[]{:S(2)}) collective-permute-start(bf16[2,2,96,384]{3,2,1,0:T(8,128)(2,1)S(1)} %fusion.8), channel_id=1, source_target_pairs={{0,4},{4,0},{8,12},{12,8},{16,20},{20,16},{24,28},{28,24},{1,5},{5... | collective-permute-start | bytes 884744 | tf_op jit(solution)/shard_map/ppermute | solution.py:632
  188.2 25.3 %collective-permute-start.31 = (bf16[2,2,96,384]{3,2,0,1:T(8,128)(2,1)S(1)}, bf16[2,2,96,384]{3,2,0,1:T(8,128)(2,1)S(1)}, u32[]{:S(2)}, u32[]{:S(2)}) collective-permute-start(bf16[2,2,96,384]{3,2,0,1:T(8,128)(2,1)S(1)} %fusion.11), channel_id=1, source_target_pairs={{0,2},{1,3},{2,0},{3,1},{4,6},{5,7},{6,4},{7,5},{8,10},{9,11},{10,... | collective-permute-start | bytes 884744 | tf_op jit(solution)/shard_map/ppermute | solution.py:632
  199.6 13.9 %collective-permute-start.33 = (bf16[2,2,96,384]{3,2,1,0:T(8,128)(2,1)S(1)}, bf16[2,2,96,384]{3,2,1,0:T(8,128)(2,1)S(1)}, u32[]{:S(2)}, u32[]{:S(2)}) collective-permute-start(bf16[2,2,96,384]{3,2,1,0:T(8,128)(2,1)S(1)} %fusion.10), channel_id=1, source_target_pairs={{0,4},{4,0},{8,12},{12,8},{16,20},{20,16},{24,28},{28,24},{1,5},{5... | collective-permute-start | bytes 884744 | tf_op jit(solution)/shard_map/ppermute | solution.py:632
  200.8 17.7 %collective-permute-start.19 = (bf16[2,2,96,384]{3,2,0,1:T(8,128)(2,1)S(1)}, bf16[2,2,96,384]{3,2,0,1:T(8,128)(2,1)S(1)}, u32[]{:S(2)}, u32[]{:S(2)}) collective-permute-start(bf16[2,2,96,384]{3,2,0,1:T(8,128)(2,1)S(1)} %fusion.13), channel_id=1, source_target_pairs={{0,2},{1,3},{2,0},{3,1},{4,6},{5,7},{6,4},{7,5},{8,10},{9,11},{10,... | collective-permute-start | bytes 884744 | tf_op jit(solution)/shard_map/ppermute | solution.py:632
  208.4 11.6 %collective-permute-start.41 = (bf16[2,2,96,384]{3,2,1,0:T(8,128)(2,1)S(1)}, bf16[2,2,96,384]{3,2,1,0:T(8,128)(2,1)S(1)}, u32[]{:S(2)}, u32[]{:S(2)}) collective-permute-start(bf16[2,2,96,384]{3,2,1,0:T(8,128)(2,1)S(1)} %pad_maximum_fusion.5), channel_id=1, source_target_pairs={{0,8},{4,12},{8,0},{12,4},{16,24},{20,28},{24,16},{28,20},{1,9},{5... | collective-permute-start | bytes 884744 | tf_op jit(solution)/shard_map/ppermute | solution.py:632
  213.7 18.4 %collective-permute-start.34 = (bf16[2,2,96,384]{3,2,1,0:T(8,128)(2,1)S(1)}, bf16[2,2,96,384]{3,2,1,0:T(8,128)(2,1)S(1)}, u32[]{:S(2)}, u32[]{:S(2)}) collective-permute-start(bf16[2,2,96,384]{3,2,1,0:T(8,128)(2,1)S(1)} %pad_maximum_fusion.3), channel_id=1, source_target_pairs={{0,8},{4,12},{8,0},{12,4},{16,24},{20,28},{24,16},{28,20},{1,9},{5... | collective-permute-start | bytes 884744 | tf_op jit(solution)/shard_map/ppermute | solution.py:632
  218.7 12.3 %collective-permute-start.22 = (bf16[2,2,96,384]{3,2,1,0:T(8,128)(2,1)S(1)}, bf16[2,2,96,384]{3,2,1,0:T(8,128)(2,1)S(1)}, u32[]{:S(2)}, u32[]{:S(2)}) collective-permute-start(bf16[2,2,96,384]{3,2,1,0:T(8,128)(2,1)S(1)} %pad_maximum_fusion.2), channel_id=1, source_target_pairs={{0,8},{4,12},{8,0},{12,4},{16,24},{20,28},{24,16},{28,20},{1,9},{5... | collective-permute-start | bytes 884744 | tf_op jit(solution)/shard_map/ppermute | solution.py:632
  220.3 24.1 %collective-permute-start.42 = (bf16[2,96,384]{2,1,0:T(8,128)(2,1)S(1)}, bf16[2,96,384]{2,1,0:T(8,128)(2,1)S(1)}, u32[]{:S(2)}, u32[]{:S(2)}) collective-permute-start(bf16[2,96,384]{2,1,0:T(8,128)(2,1)S(1)} %pad_maximum_fusion.8), channel_id=1, source_target_pairs={{0,16},{4,20},{8,24},{12,28},{16,0},{20,4},{24,8},{28,12},{1,17},{... | collective-permute-start | bytes 442376 | tf_op jit(solution)/shard_map/ppermute | solution.py:632
  231.3 12.3 %collective-permute-start.23 = (bf16[2,96,384]{2,1,0:T(8,128)(2,1)S(1)}, bf16[2,96,384]{2,1,0:T(8,128)(2,1)S(1)}, u32[]{:S(2)}, u32[]{:S(2)}) collective-permute-start(bf16[2,96,384]{2,1,0:T(8,128)(2,1)S(1)} %pad_maximum_fusion.6), channel_id=1, source_target_pairs={{0,16},{4,20},{8,24},{12,28},{16,0},{20,4},{24,8},{28,12},{1,17},{... | collective-permute-start | bytes 442376 | tf_op jit(solution)/shard_map/ppermute | solution.py:632
  232.3 13.7 %collective-permute-start.35 = (bf16[2,96,384]{2,1,0:T(8,128)(2,1)S(1)}, bf16[2,96,384]{2,1,0:T(8,128)(2,1)S(1)}, u32[]{:S(2)}, u32[]{:S(2)}) collective-permute-start(bf16[2,96,384]{2,1,0:T(8,128)(2,1)S(1)} %pad_maximum_fusion.7), channel_id=1, source_target_pairs={{0,16},{4,20},{8,24},{12,28},{16,0},{20,4},{24,8},{28,12},{1,17},{... | collective-permute-start | bytes 442376 | tf_op jit(solution)/shard_map/ppermute | solution.py:632
  (51 other events, 290.6 us)
